TPU v7x, 32 devices: a whole 2x2x4 slice. The times are simulated.
32 devices in a mesh: seq: 8 (over z, y), head: 4 (over x, core).
Axes of the slice: x: 2, y: 2, z: 4, core: 2. Of those that a mesh axis runs over, the one named last changes fastest.
Arguments:
- x_raw: bfloat16 [2048, 4096], P('seq', 'head'), may hold values from -6 to 6
- bc_raw: bfloat16 [2048, 256], P('seq'), may hold values from -6 to 6
- gate_z: bfloat16 [2048, 4096], P('seq', 'head'), may hold values from -6 to 6
- step_size: float32 [2048, 64], P('seq', 'head'), may hold values from 0.002 to 0.05
- log_decay: float32 [2048, 64], P('seq', 'head'), may hold values from -1 to 0, as said below
- doc_ids: int32 [2048], P('seq'), may hold values from 0 to 3, as said below
- conv_x: float32 [4, 4096], P(None, 'head'), may hold values from -3 to 3
- conv_bc: float32 [4, 256], replicated, may hold values from -3 to 3
- skip: float32 [64], P('head'), may hold values from 0.5 to 2
- norm_gain: float32 [4096], P('head'), may hold values from 0.25 to 1.75
Outputs:
- mixed: bfloat16 [2048, 4096], P('seq', 'head')
Inputs may be any that keep to these rules, and one draw needn't show every extreme that they name: `doc_ids`: document ids never fall along the sequence; each document has 1 to 1024 tokens, one exactly 1024. `log_decay`: every entry is negative.
All inputs are finite; a program needn't handle non-finite values.
Results may differ from a plain program's by a relative error of at most 0.005.
Values may be sent and summed in bfloat16 or wider, within the bound.
A program may use at most 192 MiB of HBM per device.

v0:
```python
import jax
import jax.numpy as jnp
from jax import lax
from jax.sharding import PartitionSpec as P

GROUP = 256


EPS = 1e-05


def shifted(block, axis, distance):
    devices = range(lax.axis_size(axis))
    route = [(i - distance, i) for i in devices if i - distance in devices]
    return lax.ppermute(block, axis, route)


def body(x_raw, bc_raw, gate_z, step_size, log_decay, doc_ids, conv_x, conv_bc, skip, norm_gain):
    rows_dev, head_cols = x_raw.shape
    heads_dev = step_size.shape[1]
    head_size = head_cols // heads_dev
    states = bc_raw.shape[1] // 2
    taps = conv_x.shape[0]
    raw_all = jnp.concatenate([x_raw, bc_raw], axis=1)
    labels = doc_ids + 1
    edge_rows = shifted(raw_all[rows_dev - (taps - 1) :], "seq", 1)
    edge_docs = shifted(labels[rows_dev - (taps - 1) :], "seq", 1)
    extended = jnp.concatenate([edge_rows, raw_all], axis=0)
    ext_docs = jnp.concatenate([edge_docs, labels], axis=0)
    kernel = jnp.concatenate([conv_x, conv_bc], axis=1)
    total = jnp.zeros(raw_all.shape, jnp.float32)
    for k in range(taps):
        moved = extended[taps - 1 - k : taps - 1 - k + rows_dev].astype(jnp.float32)
        keep = (ext_docs[taps - 1 - k : taps - 1 - k + rows_dev] == labels).astype(jnp.float32)
        total = total + kernel[k][None, :] * moved * keep[:, None]
    activated = jax.nn.silu(total).astype(jnp.bfloat16)
    xconv = activated[:, :head_cols].reshape(rows_dev, heads_dev, head_size)
    bconv = activated[:, head_cols : head_cols + states]
    cconv = activated[:, head_cols + states :]
    xdt = (xconv.astype(jnp.float32) * step_size[:, :, None]).astype(jnp.bfloat16)
    lower = jnp.arange(GROUP)[:, None] >= jnp.arange(GROUP)[None, :]
    previous = edge_docs[taps - 2] - 1
    local_in = []
    running = jnp.zeros((heads_dev, head_size, states), jnp.float32)
    through_all = jnp.ones((heads_dev,), jnp.float32)
    cum = jnp.cumsum(log_decay, axis=0)
    gram = jnp.dot(cconv, bconv.T, preferred_element_type=jnp.float32)
    mask = ((doc_ids[:, None] == doc_ids[None, :]) & lower)[None]
    diff = cum.T[:, :, None] - cum.T[:, None, :]
    weights = (jnp.where(mask, jnp.exp(jnp.where(mask, diff, 0.0)), 0.0) * gram[None]).astype(
        jnp.bfloat16
    )
    inners = jnp.einsum("hts,shp->thp", weights, xdt, preferred_element_type=jnp.float32)
    cont = (doc_ids == previous).astype(jnp.float32)
    entries = jnp.exp(cum) * cont[:, None]
    ends = jnp.where((doc_ids == doc_ids[-1])[:, None], jnp.exp(cum[-1][None, :] - cum), 0.0)
    written = (xdt.astype(jnp.float32) * ends[:, :, None]).astype(jnp.bfloat16)
    local = jnp.einsum("shp,sn->hpn", written, bconv, preferred_element_type=jnp.float32)
    local_in.append(running)
    before = through_all
    through = jnp.exp(cum[-1]) * cont[-1]
    running = through[:, None, None] * running + local
    through_all = through_all * through
    length = lax.axis_size("seq")
    hops = min(length - 1, min(16 * rows_dev, rows_dev * length // 2) // rows_dev)

    def relay_step(step, incoming):
        leaving = through_all[:, None, None] * incoming + running
        return shifted(leaving, "seq", 1)

    incoming = lax.fori_loop(0, hops, relay_step, jnp.zeros_like(running))
    entered = (before[:, None, None] * incoming).astype(jnp.bfloat16)
    carried = (
        jnp.einsum("tn,hpn->thp", cconv, entered, preferred_element_type=jnp.float32)
        * entries[:, :, None]
    )
    scanned = inners + carried + skip[None, :, None] * xconv.astype(jnp.float32)
    gated_rows = scanned.reshape(GROUP, head_cols) * jax.nn.silu(gate_z.astype(jnp.float32))
    squares = lax.psum(jnp.sum(gated_rows * gated_rows, axis=1), "head")
    scale = lax.rsqrt(squares / (head_cols * lax.axis_size("head")) + EPS)
    return (gated_rows * scale[:, None] * norm_gain[None, :]).astype(jnp.bfloat16)


def solution(mesh):
    return jax.shard_map(
        body,
        mesh=mesh,
        in_specs=(
            P("seq", "head"),
            P("seq", None),
            P("seq", "head"),
            P("seq", "head"),
            P("seq", "head"),
            P("seq"),
            P(None, "head"),
            P(),
            P("head"),
            P("head"),
        ),
        out_specs=P("seq", "head"),
        check_vma=False,
    )
```

profile of v0, /device:TPU:25, one launch (start us, length us, event | category | flops | bytes accessed | tf_op | source)
XLA Modules:
  0.0 87.2 jit_solution(18343718459737017682)
XLA Ops:
  0.0 0.7 broadcast_add_fusion
  0.8 3.1 %collective-permute-start.2 = (s32[3]{0:T(128)S(1)}, s32[3]{0:T(128)S(1)}, u32[]{:S(2)}, u32[]{:S(2)}) collective-permute-start(s32[3]{0:T(128)S(1)} %slice.68), channel_id=1, source_target_pairs={{0,4},{4,8},{8,12},{12,16},{16,20},{20,24},{24,28},{1,5},{5,9},{9,... | collective-permute-start | bytes 44 | tf_op jit(solution)/shard_map/ppermute | solution.py:15
  4.0 1.1 %constant_dynamic-update-slice_fusion.3 = bf16[256,1280]{1,0:T(8,128)(2,1)S(1)} fusion(bf16[256,1024]{1,0:T(8,128)(2,1)} %param.12), kind=kLoop, calls=%fused_computation.50 | loop fusion | bytes 1048576
  5.1 1.9 %collective-permute-start.1 = (bf16[3,1280]{1,0:T(4,128)(2,1)S(1)}, bf16[3,1280]{1,0:T(4,128)(2,1)S(1)}, u32[]{:S(2)}, u32[]{:S(2)}) collective-permute-start(bf16[3,1280]{1,0:T(4,128)(2,1)S(1)} %slice.87), channel_id=1, source_target_pairs={{0,4},{4,8},{8,12},{12,16},{16,20},{20,24},{24,28},{1,5},{5,9},{9,... | collective-permute-start | bytes 23048 | tf_op jit(solution)/shard_map/ppermute | solution.py:15
  7.1 0.6 slice.84
  7.9 0.6 reduce-window.6
  8.7 0.2 slice_reduce_fusion.1
  8.9 0.7 slice.82
  10.4 0.7 compare_convert_fusion.3
  11.1 0.6 slice.83
  11.8 0.7 broadcast_multiply_fusion
  12.4 1.2 %multiply_convert_fusion.4 = bf16[256,1280]{1,0:T(8,128)(2,1)S(1)} fusion(bf16[256,1280]{1,0:T(8,128)(2,1)S(1)} %constant_dynamic-update-slice_fusion.2, bf16[3,1280]{1,0:T(4,128)(2,1)S(1)} %collective-permute-done.1, f32[256]{0:T(256)S(1)} %get-tuple-element.47, f32[1280]{0:T(1024)S(1)} %get-tuple-element.29, f32[256]{0:T(256)S(1)} %get-tuple-element.48, ...), kind=kLoop, calls=%fused_computation.14 | loop fusion | flops 9175040 | bytes 1341952 | tf_op jit(solution)/shard_map/convert_element_type | solution.py:36
  13.8 0.2 fusion.21
  14.0 0.3 copy.22
  14.3 0.4 copy-done.3
  14.7 0.3 convolution_add_fusion
  15.0 2.3 %fusion.6 = f32[256,16,64]{0,2,1:T(8,128)} fusion(f32[256,256]{1,0:T(8,128)S(1)} %fusion.21, f32[16,256]{1,0:T(8,128)S(1)} %get-tuple-element.45, pred[256,256]{1,0:T(8,128)(4,1)S(1)} %fusion.17, f32[256,16,64]{0,2,1:T(8,128)S(1)} %bitcast.36, f32[256,16]{0,1:T(8,128)S(1)} %copy-done.3), kind=kOutput, calls=%fused_computation.8 | convolution fusion | flops 139984896 | bytes 2457600 | tf_op jit(solution)/shard_map/hts,shp->thp/dot_general | solution.py:53
  17.4 56.0 %while.10 = (s32[]{:T(128)}, f32[16,64,128]{2,1,0:T(8,128)S(1)}, f32[16]{0:T(128)S(1)}, f32[16,64,128]{2,1,0:T(8,128)S(1)}, s32[]{:T(128)}) while((s32[]{:T(128)}, f32[16,64,128]{2,1,0:T(8,128)S(1)}, f32[16]{0:T(128)S(1)}, f32[16,64,128]{2,1,0:T(8,128)S(1)}, s32[]{:T(128)}) %tuple.28), condition=%wide.region_3.4_spmd, body=%wide.region_2.3_spmd.sunk | while | flops 262146 | bytes 3670181 | solution.py:71
  17.5 1.9 %collective-permute-start = (f32[16,64,128]{2,1,0:T(8,128)S(1)}, f32[16,64,128]{2,1,0:T(8,128)S(1)}, u32[]{:S(2)}, u32[]{:S(2)}) collective-permute-start(f32[16,64,128]{2,1,0:T(8,128)S(1)} %multiply_add_fusion.2), channel_id=1, source_target_pairs={{0,4},{4,8},{8,12},{12,16},{16,20},{20,24},{24,28},{1,5},{5,9},{9,... | collective-permute-start | bytes 1572872 | tf_op jit(solution)/shard_map/while/body/eval_jaxpr/ppermute | solution.py:15
  19.5 13.3 %collective-permute-done = f32[16,64,128]{2,1,0:T(8,128)S(1)} collective-permute-done((f32[16,64,128]{2,1,0:T(8,128)S(1)}, f32[16,64,128]{2,1,0:T(8,128)S(1)}, u32[]{:S(2)}, u32[]{:S(2)}) %collective-permute-start) | collective-permute-done | bytes 524320 | tf_op jit(solution)/shard_map/while/body/eval_jaxpr/ppermute | solution.py:15
  32.9 1.9 %collective-permute-start = (f32[16,64,128]{2,1,0:T(8,128)S(1)}, f32[16,64,128]{2,1,0:T(8,128)S(1)}, u32[]{:S(2)}, u32[]{:S(2)}) collective-permute-start(f32[16,64,128]{2,1,0:T(8,128)S(1)} %multiply_add_fusion.2), channel_id=1, source_target_pairs={{0,4},{4,8},{8,12},{12,16},{16,20},{20,24},{24,28},{1,5},{5,9},{9,... | collective-permute-start | bytes 1572872 | tf_op jit(solution)/shard_map/while/body/eval_jaxpr/ppermute | solution.py:15
  34.8 12.4 %collective-permute-done = f32[16,64,128]{2,1,0:T(8,128)S(1)} collective-permute-done((f32[16,64,128]{2,1,0:T(8,128)S(1)}, f32[16,64,128]{2,1,0:T(8,128)S(1)}, u32[]{:S(2)}, u32[]{:S(2)}) %collective-permute-start) | collective-permute-done | bytes 524320 | tf_op jit(solution)/shard_map/while/body/eval_jaxpr/ppermute | solution.py:15
  47.4 1.9 %collective-permute-start = (f32[16,64,128]{2,1,0:T(8,128)S(1)}, f32[16,64,128]{2,1,0:T(8,128)S(1)}, u32[]{:S(2)}, u32[]{:S(2)}) collective-permute-start(f32[16,64,128]{2,1,0:T(8,128)S(1)} %multiply_add_fusion.2), channel_id=1, source_target_pairs={{0,4},{4,8},{8,12},{12,16},{16,20},{20,24},{24,28},{1,5},{5,9},{9,... | collective-permute-start | bytes 1572872 | tf_op jit(solution)/shard_map/while/body/eval_jaxpr/ppermute | solution.py:15
  49.3 11.5 %collective-permute-done = f32[16,64,128]{2,1,0:T(8,128)S(1)} collective-permute-done((f32[16,64,128]{2,1,0:T(8,128)S(1)}, f32[16,64,128]{2,1,0:T(8,128)S(1)}, u32[]{:S(2)}, u32[]{:S(2)}) %collective-permute-start) | collective-permute-done | bytes 524320 | tf_op jit(solution)/shard_map/while/body/eval_jaxpr/ppermute | solution.py:15
  60.9 1.9 %collective-permute-start = (f32[16,64,128]{2,1,0:T(8,128)S(1)}, f32[16,64,128]{2,1,0:T(8,128)S(1)}, u32[]{:S(2)}, u32[]{:S(2)}) collective-permute-start(f32[16,64,128]{2,1,0:T(8,128)S(1)} %multiply_add_fusion.2), channel_id=1, source_target_pairs={{0,4},{4,8},{8,12},{12,16},{16,20},{20,24},{24,28},{1,5},{5,9},{9,... | collective-permute-start | bytes 1572872 | tf_op jit(solution)/shard_map/while/body/eval_jaxpr/ppermute | solution.py:15
  62.8 10.6 %collective-permute-done = f32[16,64,128]{2,1,0:T(8,128)S(1)} collective-permute-done((f32[16,64,128]{2,1,0:T(8,128)S(1)}, f32[16,64,128]{2,1,0:T(8,128)S(1)}, u32[]{:S(2)}, u32[]{:S(2)}) %collective-permute-start) | collective-permute-done | bytes 524320 | tf_op jit(solution)/shard_map/while/body/eval_jaxpr/ppermute | solution.py:15
  73.4 1.5 %fusion.8 = f32[256,16,64]{0,2,1:T(8,128)S(1)} fusion(f32[256,16,64]{0,2,1:T(8,128)} %fusion.6, f32[256,16,64]{0,2,1:T(8,128)S(1)} %bitcast.37, f32[16]{0:T(128)S(1)} %copy-done.8, f32[256,16]{0,1:T(8,128)S(1)} %get-tuple-element.43, f32[16,64,128]{2,1,0:T(8,128)S(1)} %get-tuple-element.27, bf16[256,1280]{1,0:T(8,128)(2,1)S(1)} %multiply_convert_fusion.4), kind=kOutput, calls=%fused_computation.11 | convolution fusion | flops 68288512 | bytes 3752448 | tf_op jit(solution)/shard_map/tn,hpn->thp/dot_general | solution.py:74
  75.0 0.3 copy.25
  75.3 0.7 copy-done.1
  76.0 0.4 multiply_reduce_fusion
  76.4 9.6 %psum.7 = f32[256]{0:T(256)S(1)} all-reduce(f32[256]{0:T(256)S(1)} %multiply_reduce_fusion), channel_id=1, replica_groups=mesh['seq'=8,'head'=4] {'head'}, use_global_device_ids=true, to_apply=%region_5.6 | all-reduce | flops 256 | bytes 2048 | tf_op jit(solution)/shard_map/psum | solution.py:79
  86.0 1.2 %multiply_convert_fusion.5 = bf16[256,1024]{1,0:T(8,128)(2,1)} fusion(f32[1024]{0:T(1024)S(1)} %copy-done.6, f32[256]{0:T(256)S(1)} %add_rsqrt_fusion, f32[256,1024]{1,0:T(8,128)S(1)} %copy.25, bf16[256,1024]{1,0:T(8,128)(2,1)S(1)} %copy-done.1), kind=kLoop, calls=%fused_computation.20 | loop fusion | flops 2359296 | bytes 2102272 | tf_op jit(solution)/shard_map/convert_element_type | solution.py:81
  (39 shorter events, 1.4 us)
Async XLA Ops:
  0.0 7.9 %copy-start = (f32[256,16]{0,1:T(8,128)S(1)}, f32[256,16]{0,1:T(8,128)}, u32[]{:S(2)}) copy-start(f32[256,16]{0,1:T(8,128)} %param.16) | copy-start | bytes 49156
  0.0 7.0 %copy-start.4 = (s32[256]{0:T(256)S(1)}, s32[256]{0:T(256)}, u32[]{:S(2)}) copy-start(s32[256]{0:T(256)} %param.17) | copy-start | bytes 3076
  0.0 5.1 %copy-start.2 = (bf16[256,256]{1,0:T(8,128)(2,1)S(1)}, bf16[256,256]{1,0:T(8,128)(2,1)}, u32[]{:S(2)}) copy-start(bf16[256,256]{1,0:T(8,128)(2,1)} %param.13) | copy-start | bytes 393220
  0.0 7.7 %copy-start.5 = (f32[4,1024]{1,0:T(4,128)S(1)}, f32[4,1024]{1,0:T(4,128)}, u32[]{:S(2)}) copy-start(f32[4,1024]{1,0:T(4,128)} %param.18) | copy-start | bytes 49156
  0.0 7.7 %copy-start.7 = (f32[4,256]{1,0:T(4,128)S(1)}, f32[4,256]{1,0:T(4,128)}, u32[]{:S(2)}) copy-start(f32[4,256]{1,0:T(4,128)} %param.19) | copy-start | bytes 12292
  0.8 8.1 %collective-permute-start.2 = (s32[3]{0:T(128)S(1)}, s32[3]{0:T(128)S(1)}, u32[]{:S(2)}, u32[]{:S(2)}) collective-permute-start(s32[3]{0:T(128)S(1)} %slice.68), channel_id=1, source_target_pairs={{0,4},{4,8},{8,12},{12,16},{16,20},{20,24},{24,28},{1,5},{5,9},{9,... | collective-permute-start | bytes 44 | tf_op jit(solution)/shard_map/ppermute | solution.py:15
  5.1 7.3 %collective-permute-start.1 = (bf16[3,1280]{1,0:T(4,128)(2,1)S(1)}, bf16[3,1280]{1,0:T(4,128)(2,1)S(1)}, u32[]{:S(2)}, u32[]{:S(2)}) collective-permute-start(bf16[3,1280]{1,0:T(4,128)(2,1)S(1)} %slice.87), channel_id=1, source_target_pairs={{0,4},{4,8},{8,12},{12,16},{16,20},{20,24},{24,28},{1,5},{5,9},{9,... | collective-permute-start | bytes 23048 | tf_op jit(solution)/shard_map/ppermute | solution.py:15
  14.0 0.7 copy-start.3
  17.4 56.0 %copy-start.8 = (f32[16]{0:T(128)S(1)}, f32[16]{0:T(128)}, u32[]{:S(2)}) copy-start(f32[16]{0:T(128)} %param.20) | copy-start | bytes 196
  17.5 15.3 %collective-permute-start = (f32[16,64,128]{2,1,0:T(8,128)S(1)}, f32[16,64,128]{2,1,0:T(8,128)S(1)}, u32[]{:S(2)}, u32[]{:S(2)}) collective-permute-start(f32[16,64,128]{2,1,0:T(8,128)S(1)} %multiply_add_fusion.2), channel_id=1, source_target_pairs={{0,4},{4,8},{8,12},{12,16},{16,20},{20,24},{24,28},{1,5},{5,9},{9,... | collective-permute-start | bytes 1572872 | tf_op jit(solution)/shard_map/while/body/eval_jaxpr/ppermute | solution.py:15
  32.9 14.3 %collective-permute-start = (f32[16,64,128]{2,1,0:T(8,128)S(1)}, f32[16,64,128]{2,1,0:T(8,128)S(1)}, u32[]{:S(2)}, u32[]{:S(2)}) collective-permute-start(f32[16,64,128]{2,1,0:T(8,128)S(1)} %multiply_add_fusion.2), channel_id=1, source_target_pairs={{0,4},{4,8},{8,12},{12,16},{16,20},{20,24},{24,28},{1,5},{5,9},{9,... | collective-permute-start | bytes 1572872 | tf_op jit(solution)/shard_map/while/body/eval_jaxpr/ppermute | solution.py:15
  47.4 13.4 %collective-permute-start = (f32[16,64,128]{2,1,0:T(8,128)S(1)}, f32[16,64,128]{2,1,0:T(8,128)S(1)}, u32[]{:S(2)}, u32[]{:S(2)}) collective-permute-start(f32[16,64,128]{2,1,0:T(8,128)S(1)} %multiply_add_fusion.2), channel_id=1, source_target_pairs={{0,4},{4,8},{8,12},{12,16},{16,20},{20,24},{24,28},{1,5},{5,9},{9,... | collective-permute-start | bytes 1572872 | tf_op jit(solution)/shard_map/while/body/eval_jaxpr/ppermute | solution.py:15
  60.9 12.5 %collective-permute-start = (f32[16,64,128]{2,1,0:T(8,128)S(1)}, f32[16,64,128]{2,1,0:T(8,128)S(1)}, u32[]{:S(2)}, u32[]{:S(2)}) collective-permute-start(f32[16,64,128]{2,1,0:T(8,128)S(1)} %multiply_add_fusion.2), channel_id=1, source_target_pairs={{0,4},{4,8},{8,12},{12,16},{16,20},{20,24},{24,28},{1,5},{5,9},{9,... | collective-permute-start | bytes 1572872 | tf_op jit(solution)/shard_map/while/body/eval_jaxpr/ppermute | solution.py:15
  74.9 1.0 %copy-start.1 = (bf16[256,1024]{1,0:T(8,128)(2,1)S(1)}, bf16[256,1024]{1,0:T(8,128)(2,1)}, u32[]{:S(2)}) copy-start(bf16[256,1024]{1,0:T(8,128)(2,1)} %param.14) | copy-start | bytes 1572868
  76.0 10.1 %copy-start.6 = (f32[1024]{0:T(1024)S(1)}, f32[1024]{0:T(1024)}, u32[]{:S(2)}) copy-start(f32[1024]{0:T(1024)} %param.21) | copy-start | bytes 12292
where the time goes:
time: 88.3 us; the launch traced here: 87.2 us
  waiting for transfers between devices  47.8 us (54%)
  starting transfers between devices  12.7 us (14%)
  blocking collectives  9.65 us (11%)
  other arithmetic  6.45 us (7%)
  local copies, waits for them, and re-layouts  5.23 us (6%)
  matrix products  4.34 us (5%)
  between operations  0.94 us (1%)
    ppermute x6, waiting for transfers between devices, shifted(): return lax.ppermute(block, axis, route)  47.8 us
    ppermute x6, starting transfers between devices, shifted(): return lax.ppermute(block, axis, route)  12.7 us
    psum x1, blocking collectives, body(): squares = lax.psum(jnp.sum(gated_rows * gated_rows, axis=1), 'head')  9.65 us
    dot_general x1, matrix products, body(): jnp.einsum('hts,shp->thp', weights, xdt, preferred_element_type=jnp.float32)  2.32 us
    unnamed x20, local copies, waits for them, and re-layouts  2.18 us
  transfers between devices with their start and end apart: 6, of which 4 were waited for; matrix products, arithmetic and copies ran while one was open for 7% of the time, Pallas kernels for 0%

commit v1 on v0

v1 whole, which is shorter than its diff:
```python
import functools

import jax
import jax.numpy as jnp
from jax import lax
from jax.experimental import pallas as pl
from jax.experimental.pallas import tpu as pltpu
from jax.sharding import PartitionSpec as P

EPS = 1e-05
MESH = pl.DeviceIdType.MESH
F32 = jnp.float32
BF16 = jnp.bfloat16
LANES = 128
TAIL = 16


def dot(a, b):
    return jnp.dot(a, b, preferred_element_type=F32)


def split2(v):
    high = v.astype(BF16)
    return high, (v - high.astype(F32)).astype(BF16)


def split3(v):
    high, _ = split2(v)
    mid, low = split2(v - high.astype(F32))
    return high, mid, low


def silu(v):
    return v / (1.0 + jnp.exp(-v))


def kernel(
    length, groups,
    x, bc, z, step, decay, docs, taps_x, taps_bc, skip, gain,
    out,
    xc, bcc, base, enter_scale, write_scale, local,
    edge_x, edge_bc, edge_docs,
    pair_out, pair_in, chain_out, chain_in, share_out, share_in, own_entered,
    squares_out, squares_in,
    edge_send, edge_recv, pair_send, pair_recv, chain_send, chain_recv,
    share_send, share_recv, squares_send, squares_recv,
):
    rows, cols = x.shape
    heads = step.shape[1]
    size = cols // heads
    states = bc.shape[1] // 2
    slabs = cols // LANES
    half = slabs // 2
    taps = taps_x.shape[0]
    me = lax.axis_index("seq")
    group = lax.axis_index("head")
    odd = me % 2
    partner = me + 1 - 2 * odd
    peers = [(group + d) % groups for d in range(1, groups)]

    barrier = pltpu.get_barrier_semaphore()
    near = (
        (me > 0, me - 1), (me < length - 1, me + 1), (me > 1, me - 2), (me < length - 2, me + 2),
    )

    for present, other in near:
        @pl.when(present)
        def _(other=other):
            pl.semaphore_signal(barrier, inc=1, device_id=(other, group), device_id_type=MESH)
    for peer in peers:
        pl.semaphore_signal(barrier, inc=1, device_id=(me, peer), device_id_type=MESH)

    def remote(src, dst, send, recv, seq, head):
        return pltpu.make_async_remote_copy(
            src_ref=src, dst_ref=dst, send_sem=send, recv_sem=recv,
            device_id=(seq, head), device_id_type=MESH,
        )

    after = length - 1 - me
    callers = groups - 1
    for position in (me, after):
        callers = callers + (position + length - 1) // length + (position + length - 2) // length
    pl.semaphore_wait(barrier, callers)

    edges = [
        remote(x.at[pl.ds(rows - TAIL, TAIL)], edge_x, edge_send.at[0], edge_recv.at[0], me + 1, group),
        remote(bc.at[pl.ds(rows - TAIL, TAIL)], edge_bc, edge_send.at[1], edge_recv.at[1], me + 1, group),
        remote(docs, edge_docs, edge_send.at[2], edge_recv.at[2], me + 1, group),
    ]

    @pl.when(me < length - 1)
    def _():
        for copy in edges:
            copy.start()

    @pl.when(me == 0)
    def _():
        edge_x[...] = jnp.zeros_like(edge_x)
        edge_bc[...] = jnp.zeros_like(edge_bc)
        edge_docs[...] = jnp.full(edge_docs.shape, -1, jnp.int32)

    doc_row = docs[...].astype(F32)
    doc_col = jnp.transpose(jnp.broadcast_to(doc_row, (LANES, rows)))
    same = jnp.concatenate([doc_col] * (rows // LANES), axis=1) == jnp.broadcast_to(doc_row, (rows, rows))
    gap = lax.broadcasted_iota(jnp.int32, (rows, rows), 0) - lax.broadcasted_iota(jnp.int32, (rows, rows), 1)
    lower = jnp.where(gap >= 0, 1.0, 0.0).astype(BF16)
    moves = [jnp.where(same & (gap == k), 1.0, 0.0).astype(BF16) for k in range(1, taps)]

    def conv(raw, weights, shifts, source):
        total = weights[0:1] * raw.astype(F32)
        for k in range(1, taps):
            total = total + weights[k : k + 1] * dot(shifts[k - 1], source)
        return silu(total).astype(BF16)

    cum = sum(dot(lower, part) for part in split3(decay[...]))
    doc_heads = doc_col[:, :heads]
    ends = jnp.where(doc_heads == doc_row[:, rows - 1 :], jnp.exp(cum[rows - 1 :] - cum), 0.0)
    spread = jnp.where(
        lax.broadcasted_iota(jnp.int32, (2 * heads, cols), 0) % heads
        == lax.broadcasted_iota(jnp.int32, (2 * heads, cols), 1) // size,
        1.0, 0.0,
    ).astype(BF16)

    def widen(v):
        return dot(jnp.concatenate(split2(v), axis=1), spread)

    write_scale[...] = widen(step[...] * ends)
    skip_row = widen(jnp.broadcast_to(skip[...], (8, heads)))[0:1]
    minus = jnp.transpose(cum - jnp.log(step[...]))

    bcc[...] = conv(bc[...], taps_bc[...], moves, bc[...])
    wide = 2 * LANES
    for j in range(cols // wide):
        part = pl.ds(j * wide, wide)
        xc[:, part] = conv(x[:, part], taps_x[:, part], moves, x[:, part])

    @pl.when(me > 0)
    def _():
        for copy in edges:
            copy.wait_recv()

    before = edge_docs[...].astype(F32)
    first = jnp.concatenate([before[:, rows - TAIL :], doc_row[:, :TAIL]], axis=1)
    first_gap = (
        lax.broadcasted_iota(jnp.int32, (TAIL, 2 * TAIL), 0)
        + TAIL
        - lax.broadcasted_iota(jnp.int32, (TAIL, 2 * TAIL), 1)
    )
    first_same = doc_col[:TAIL, : 2 * TAIL] == jnp.broadcast_to(first, (TAIL, 2 * TAIL))
    first_moves = [
        jnp.where(first_same & (first_gap == k), 1.0, 0.0).astype(BF16) for k in range(1, taps)
    ]
    head_bc = bc[:TAIL]
    bcc[:TAIL] = conv(head_bc, taps_bc[...], first_moves, jnp.concatenate([edge_bc[...], head_bc], axis=0))
    head_x = x[:TAIL]
    xc[:TAIL] = conv(head_x, taps_x[...], first_moves, jnp.concatenate([edge_x[...], head_x], axis=0))

    enter_scale[...] = widen(jnp.where(doc_heads == before[:, rows - 1 :], jnp.exp(cum), 0.0))
    b_turned = jnp.transpose(bcc[:, :states].astype(F32)).astype(BF16)
    c_rows = bcc[:, states:]

    def slab(k):
        return pl.ds(pl.multiple_of(k * LANES, LANES), LANES)

    def local_state(k):
        written = (xc[:, slab(k)].astype(F32) * write_scale[:, slab(k)]).astype(BF16)
        return dot(b_turned, written)

    pairs, chains, shares = [], [], []
    for c in range(half):
        k = (1 - odd) * half + c
        pair_out[c, :states] = local_state(k).astype(BF16)
        through = jnp.broadcast_to(enter_scale[rows - 8 :, slab(k)][7:8], (TAIL, LANES))
        high, low = split2(through)
        kind = lax.broadcasted_iota(jnp.int32, (TAIL, LANES), 0)
        pair_out[c, states:] = jnp.where(kind < 8, high.astype(F32), low.astype(F32)).astype(BF16)
        pairs.append(remote(pair_out.at[c], pair_in.at[c], pair_send.at[c], pair_recv.at[c], partner, group))
        chains.append(remote(chain_out.at[c], chain_in.at[c], chain_send.at[c], chain_recv.at[c], me + 2, group))
        shares.append(remote(share_out.at[c], share_in.at[c], share_send.at[c], share_recv.at[c], partner, group))
        pairs[c].start()
    for c in range(half):
        local[c] = local_state(odd * half + c)

    @pl.when(me < 2)
    def _():
        chain_in[...] = jnp.zeros_like(chain_in)

    gram = jnp.where(same & (gap >= 0), dot(c_rows, b_turned), 0.0)
    mid = rows // 2
    lane = lax.broadcasted_iota(jnp.int32, (rows, LANES), 1)
    per_slab = LANES // size
    for j in range(slabs):
        part = pl.ds(j * LANES, LANES)
        values = xc[:, part]
        inner = None
        for i in range(per_slab):
            h = j * per_slab + i
            at = cum[:, h : h + 1]
            minus_row = minus[h : h + 1]
            upper = gram[:mid, :mid] * jnp.exp(jnp.minimum(at[:mid] - minus_row[:, :mid], 0.0))
            left = gram[mid:, :mid] * jnp.exp(at[mid:] - minus_row[:, :mid])
            right = gram[mid:, mid:] * jnp.exp(jnp.minimum(at[mid:] - minus_row[:, mid:], 0.0))
            below = jnp.concatenate([left.astype(BF16), right.astype(BF16)], axis=1)
            term = jnp.concatenate([dot(upper.astype(BF16), values[:mid]), dot(below, values)], axis=0)
            inner = term if inner is None else jnp.where(lane < i * size, inner, term)
        gate = silu(z[:, part].astype(F32))
        base[:, part] = (inner + skip_row[:, j * LANES : (j + 1) * LANES] * values.astype(F32)) * gate
        own_through = enter_scale[rows - 8 :, part]
        enter_scale[: rows - 8, part] = enter_scale[: rows - 8, part] * gate[: rows - 8]
        enter_scale[rows - 8 :, part] = own_through * gate[rows - 8 :]

    is_odd = jnp.full((states, LANES), odd, jnp.int32) == 1
    through_row = widen(
        jnp.broadcast_to(
            jnp.where(doc_heads[rows - 1 :] == before[:, rows - 1 :], jnp.exp(cum[rows - 1 :]), 0.0),
            (8, heads),
        )
    )[0:1]
    for c in range(half):
        pairs[c].wait_recv()
        mine = local[c]
        theirs = pair_in[c, :states].astype(F32)
        extra = pair_in[c, states:].astype(F32)
        their_through = jnp.broadcast_to(extra[0:1] + extra[8:9], (states, LANES))
        own_half = [through_row[:, (s * half + c) * LANES : (s * half + c + 1) * LANES] for s in (0, 1)]
        my_through = jnp.where(
            is_odd,
            jnp.broadcast_to(own_half[1], (states, LANES)),
            jnp.broadcast_to(own_half[0], (states, LANES)),
        )
        even_local = jnp.where(is_odd, theirs, mine)
        odd_local = jnp.where(is_odd, mine, theirs)
        even_through = jnp.where(is_odd, their_through, my_through)
        odd_through = jnp.where(is_odd, my_through, their_through)

        @pl.when(me > 1)
        def _(c=c):
            chains[c].wait_recv()

        incoming = chain_in[c].astype(F32)
        between = even_local + even_through * incoming
        chain_out[c] = (odd_local + odd_through * between).astype(BF16)

        @pl.when(me < length - 2)
        def _(c=c):
            chains[c].start()

        share_out[c] = jnp.where(is_odd, incoming, between).astype(BF16)
        shares[c].start()
        own_entered[c] = jnp.where(is_odd, between, incoming).astype(BF16)

    total = jnp.zeros((rows, LANES), F32)

    def finish(k, entered, total):
        gated = base[:, slab(k)] + dot(c_rows, entered) * enter_scale[:, slab(k)]
        base[:, slab(k)] = gated
        return total + gated * gated

    for c in range(half):
        total = finish(odd * half + c, own_entered[c], total)
    for c in range(half):
        shares[c].wait_recv()
        total = finish((1 - odd) * half + c, share_in[c], total)

    squares = jnp.sum(jnp.transpose(total), axis=0, keepdims=True)
    squares_out[...] = jnp.broadcast_to(squares, squares_out.shape)
    sums = [
        remote(squares_out, squares_in.at[d], squares_send.at[d], squares_recv.at[d], me, peer)
        for d, peer in enumerate(peers)
    ]
    for copy in sums:
        copy.start()
    for d, copy in enumerate(sums):
        copy.wait_recv()
        squares = squares + squares_in[d, 0:1]
    scale = jnp.transpose(jnp.broadcast_to(lax.rsqrt(squares / (cols * groups) + EPS), (LANES, rows)))
    for j in range(slabs):
        part = pl.ds(j * LANES, LANES)
        out[:, part] = (base[:, part] * scale * gain[:, part]).astype(BF16)

    for copy in sums + pairs + shares:
        copy.wait_send()

    @pl.when(me < length - 2)
    def _():
        for copy in chains:
            copy.wait_send()

    @pl.when(me < length - 1)
    def _():
        for copy in edges:
            copy.wait_send()


def body(x_raw, bc_raw, gate_z, step_size, log_decay, doc_ids, conv_x, conv_bc, skip, norm_gain):
    rows, cols = x_raw.shape
    states = bc_raw.shape[1] // 2
    length, groups = lax.axis_size("seq"), lax.axis_size("head")
    half = cols // LANES // 2
    dma = pltpu.SemaphoreType.DMA
    block = pltpu.VMEM((half, states, LANES), BF16)
    pair = pltpu.VMEM((half, states + TAIL, LANES), BF16)
    wide = pltpu.VMEM((rows, cols), F32)
    return pl.pallas_call(
        functools.partial(kernel, length, groups),
        out_shape=jax.ShapeDtypeStruct((rows, cols), BF16),
        in_specs=[pl.BlockSpec(memory_space=pltpu.VMEM)] * 10,
        out_specs=pl.BlockSpec(memory_space=pltpu.VMEM),
        scratch_shapes=[
            pltpu.VMEM((rows, cols), BF16),
            pltpu.VMEM((rows, 2 * states), BF16),
            wide, wide, wide,
            pltpu.VMEM((half, states, LANES), F32),
            pltpu.VMEM((TAIL, cols), BF16),
            pltpu.VMEM((TAIL, 2 * states), BF16),
            pltpu.VMEM((1, rows), jnp.int32),
            pair, pair, block, block, block, block, block,
            pltpu.VMEM((8, rows), F32),
            pltpu.VMEM((groups - 1, 8, rows), F32),
            dma((3,)), dma((3,)),
            dma((half,)), dma((half,)), dma((half,)), dma((half,)), dma((half,)), dma((half,)),
            dma((groups - 1,)), dma((groups - 1,)),
        ],
        compiler_params=pltpu.CompilerParams(
            collective_id=0, has_side_effects=True, vmem_limit_bytes=40 * 1024 * 1024
        ),
        cost_estimate=pl.CostEstimate(flops=10**9, bytes_accessed=2 * 10**6, transcendentals=10**6),
    )(
        x_raw, bc_raw, gate_z, step_size, log_decay, doc_ids.reshape(1, rows),
        conv_x, conv_bc, skip.reshape(1, -1), norm_gain.reshape(1, -1),
    )


def solution(mesh):
    return jax.shard_map(
        body,
        mesh=mesh,
        in_specs=(
            P("seq", "head"),
            P("seq", None),
            P("seq", "head"),
            P("seq", "head"),
            P("seq", "head"),
            P("seq"),
            P(None, "head"),
            P(),
            P("head"),
            P("head"),
        ),
        out_specs=P("seq", "head"),
        check_vma=False,
    )
```

time: 88.3 us -> 29.2 us (0.33)
  the two profiles are of different devices: /device:TPU:25 before, /device:TPU:29 now
where the time goes in v1:
time: 29.2 us; the launch traced here: 28.8 us
  Pallas kernels  24.3 us (83%)
  local copies, waits for them, and re-layouts  4.43 us (15%)
    pallas_call x1, Pallas kernels, body(): pl.pallas_call(functools.partial(kernel, length, groups), out_shape=jax.S...  24.3 us
    unnamed x21, local copies, waits for them, and re-layouts  4.43 us

profile of v1, /device:TPU:29, one launch (start us, length us, event | category | flops | bytes accessed | tf_op | source)
XLA Modules:
  0.0 28.8 jit_solution(13513368451183889346)
XLA Ops:
  0.0 0.0 copy-start.8
  0.0 0.0 copy-start.2
  0.0 0.9 %copy.11.step = f32[256,16]{1,0:T(8,128)S(1)} copy(f32[256,16]{0,1:T(8,128)} %param.13) | data formatting | bytes 32768 | tf_op args[3]
  0.9 0.0 copy-done.8
  0.9 0.0 copy-start.3
  0.9 0.0 copy-start.4
  0.9 0.0 copy-start.5
  0.9 0.0 copy-start.6
  0.9 0.0 copy-start.7
  0.9 0.1 copy.12.decay
  1.0 0.0 copy-done.2
  1.0 0.6 %copy-done.3 = f32[4,1024]{1,0:T(4,128)S(1)} copy-done((f32[4,1024]{1,0:T(4,128)S(1)}, f32[4,1024]{1,0:T(4,128)}, u32[]{:S(2)}) %copy-start.3) | copy-done | bytes 16408
  1.6 0.0 copy-done.4
  1.6 0.0 copy-done.5
  1.6 0.0 copy-done.6
  1.6 0.0 copy-done.7
  1.6 0.0 copy-start
  1.6 1.0 %copy-done = bf16[256,1024]{1,0:T(8,128)(2,1)S(1)} copy-done((bf16[256,1024]{1,0:T(8,128)(2,1)S(1)}, bf16[256,1024]{1,0:T(8,128)(2,1)}, u32[]{:S(2)}) %copy-start) | copy-done | bytes 524312
  2.7 0.0 copy-start.1
  2.7 1.0 %copy-done.1 = bf16[256,1024]{1,0:T(8,128)(2,1)S(1)} copy-done((bf16[256,1024]{1,0:T(8,128)(2,1)S(1)}, bf16[256,1024]{1,0:T(8,128)(2,1)}, u32[]{:S(2)}) %copy-start.1) | copy-done | bytes 524312
  3.7 24.3 %shard_map.100 = bf16[256,1024]{1,0:T(8,128)(2,1)S(1)} custom-call(bf16[256,1024]{1,0:T(8,128)(2,1)S(1)} %copy-done, bf16[256,256]{1,0:T(8,128)(2,1)S(1)} %copy-done.2, bf16[256,1024]{1,0:T(8,128)(2,1)S(1)} %copy-done.1, f32[256,16]{1,0:T(8,128)S(1)} %copy.11.step, f32[256,16]{1,0:T(8,128)S(1)} %copy.12.decay, s32[1,256]{1,0:T(1,128)S(1)} %bitcast.4, ...), custom_call_target="tpu_custom_call" | custom-call | flops 1000000000 | bytes 2000000 | tf_op jit(solution)/shard_map/pallas_call | solution.py:304
  28.0 0.8 %copy.14 = bf16[256,1024]{1,0:T(8,128)(2,1)} copy(bf16[256,1024]{1,0:T(8,128)(2,1)S(1)} %shard_map.100) | data formatting | bytes 1048576
Async XLA Ops:
  0.0 0.9 %copy-start.8 = (f32[256,16]{0,1:T(8,128)S(1)}, f32[256,16]{0,1:T(8,128)}, u32[]{:S(2)}) copy-start(f32[256,16]{0,1:T(8,128)} %param.14) | copy-start | bytes 49156
  0.0 1.0 %copy-start.2 = (bf16[256,256]{1,0:T(8,128)(2,1)S(1)}, bf16[256,256]{1,0:T(8,128)(2,1)}, u32[]{:S(2)}) copy-start(bf16[256,256]{1,0:T(8,128)(2,1)} %bc.1) | copy-start | bytes 393220
  0.9 0.7 %copy-start.3 = (f32[4,1024]{1,0:T(4,128)S(1)}, f32[4,1024]{1,0:T(4,128)}, u32[]{:S(2)}) copy-start(f32[4,1024]{1,0:T(4,128)} %taps_x.1) | copy-start | bytes 49156
  0.9 0.7 %copy-start.4 = (f32[4,256]{1,0:T(4,128)S(1)}, f32[4,256]{1,0:T(4,128)}, u32[]{:S(2)}) copy-start(f32[4,256]{1,0:T(4,128)} %taps_bc.1) | copy-start | bytes 12292
  0.9 0.7 %copy-start.5 = (f32[1024]{0:T(1024)S(1)}, f32[1024]{0:T(1024)}, u32[]{:S(2)}) copy-start(f32[1024]{0:T(1024)} %param.19) | copy-start | bytes 12292
  0.9 0.7 %copy-start.6 = (s32[256]{0:T(256)S(1)}, s32[256]{0:T(256)}, u32[]{:S(2)}) copy-start(s32[256]{0:T(256)} %param.15) | copy-start | bytes 3076
  0.9 0.7 %copy-start.7 = (f32[16]{0:T(128)S(1)}, f32[16]{0:T(128)}, u32[]{:S(2)}) copy-start(f32[16]{0:T(128)} %param.18) | copy-start | bytes 196
  1.6 1.0 %copy-start = (bf16[256,1024]{1,0:T(8,128)(2,1)S(1)}, bf16[256,1024]{1,0:T(8,128)(2,1)}, u32[]{:S(2)}) copy-start(bf16[256,1024]{1,0:T(8,128)(2,1)} %x.1) | copy-start | bytes 1572868
  2.7 1.0 %copy-start.1 = (bf16[256,1024]{1,0:T(8,128)(2,1)S(1)}, bf16[256,1024]{1,0:T(8,128)(2,1)}, u32[]{:S(2)}) copy-start(bf16[256,1024]{1,0:T(8,128)(2,1)} %z.1) | copy-start | bytes 1572868

commit v2 on v1

v2 whole, which is shorter than its diff:
```python
import functools

import jax
import jax.numpy as jnp
from jax import lax
from jax.experimental import pallas as pl
from jax.experimental.pallas import tpu as pltpu
from jax.sharding import PartitionSpec as P

EPS = 1e-05
MESH = pl.DeviceIdType.MESH
F32 = jnp.float32
BF16 = jnp.bfloat16
LANES = 128
TAIL = 16


def dot(a, b):
    return jnp.dot(a, b, preferred_element_type=F32)


def split2(v):
    high = v.astype(BF16)
    return high, (v - high.astype(F32)).astype(BF16)


def split3(v):
    high, _ = split2(v)
    mid, low = split2(v - high.astype(F32))
    return high, mid, low


def silu(v):
    return v / (1.0 + jnp.exp(-v))


def kernel(
    length, groups, rounds,
    x_far, bc_far, z_far, step, decay, docs, taps_x, taps_bc, skip, gain,
    out,
    x, bc, z, load_sem,
    xc, bcc, base, enter_scale, write_scale, local, pair_local,
    edge_x, edge_bc, edge_docs,
    pair_out, pair_in, chain_out, chain_in, share_out, share_in, own_entered,
    squares_out, squares_in,
    edge_send, edge_recv, pair_send, pair_recv, chain_send, chain_recv,
    share_send, share_recv, squares_send, squares_recv,
):
    rows, cols = x.shape
    heads = step.shape[0]
    size = cols // heads
    states = bc.shape[1] // 2
    slabs = cols // LANES
    half = slabs // 2
    taps = taps_x.shape[0]
    me = lax.axis_index("seq")
    group = lax.axis_index("head")
    odd = me % 2
    partner = me + 1 - 2 * odd
    peers = [(group + d) % groups for d in range(1, groups)]

    loads = [
        pltpu.make_async_copy(far, here, load_sem.at[i])
        for i, (far, here) in enumerate(((bc_far, bc), (x_far, x), (z_far, z)))
    ]
    for copy in loads:
        copy.start()

    barrier = pltpu.get_barrier_semaphore()
    near = (
        (me > 0, me - 1), (me < length - 1, me + 1), (me > 1, me - 2), (me < length - 2, me + 2),
    )

    for present, other in near:
        @pl.when(present)
        def _(other=other):
            pl.semaphore_signal(barrier, inc=1, device_id=(other, group), device_id_type=MESH)
    for peer in peers:
        pl.semaphore_signal(barrier, inc=1, device_id=(me, peer), device_id_type=MESH)

    def remote(src, dst, send, recv, seq, head):
        return pltpu.make_async_remote_copy(
            src_ref=src, dst_ref=dst, send_sem=send, recv_sem=recv,
            device_id=(seq, head), device_id_type=MESH,
        )

    after = length - 1 - me
    callers = groups - 1
    for position in (me, after):
        callers = callers + (position + length - 1) // length + (position + length - 2) // length
    pl.semaphore_wait(barrier, callers)

    edges = [
        remote(x_far.at[pl.ds(rows - TAIL, TAIL)], edge_x, edge_send.at[0], edge_recv.at[0], me + 1, group),
        remote(bc_far.at[pl.ds(rows - TAIL, TAIL)], edge_bc, edge_send.at[1], edge_recv.at[1], me + 1, group),
        remote(docs, edge_docs, edge_send.at[2], edge_recv.at[2], me + 1, group),
    ]

    @pl.when(me < length - 1)
    def _():
        for copy in edges:
            copy.start()

    @pl.when(me == 0)
    def _():
        edge_x[...] = jnp.zeros_like(edge_x)
        edge_bc[...] = jnp.zeros_like(edge_bc)
        edge_docs[...] = jnp.full(edge_docs.shape, -1, jnp.int32)

    doc_row = docs[...].astype(F32)
    doc_col = jnp.transpose(jnp.broadcast_to(doc_row, (LANES, rows)))
    same = jnp.concatenate([doc_col] * (rows // LANES), axis=1) == jnp.broadcast_to(doc_row, (rows, rows))
    gap = lax.broadcasted_iota(jnp.int32, (rows, rows), 0) - lax.broadcasted_iota(jnp.int32, (rows, rows), 1)
    upper = jnp.where(gap <= 0, 1.0, 0.0).astype(BF16)
    moves = [jnp.where(same & (gap == k), 1.0, 0.0).astype(BF16) for k in range(1, taps)]

    def conv(raw, weights, shifts, source):
        total = weights[0:1] * raw.astype(F32)
        for k in range(1, taps):
            total = total + weights[k : k + 1] * dot(shifts[k - 1], source)
        return silu(total).astype(BF16)

    parts = dot(jnp.concatenate(split3(decay[...]), axis=0), upper)
    cum_rows = parts[:heads] + parts[heads : 2 * heads] + parts[2 * heads :]
    cum_last = cum_rows[:, rows - 1 :]
    ends = jnp.where(doc_row == doc_row[:, rows - 1 :], jnp.exp(cum_last - cum_rows), 0.0)
    minus = cum_rows - jnp.log(step[...])
    spread = jnp.where(
        lax.broadcasted_iota(jnp.int32, (2 * heads, cols), 0) % heads
        == lax.broadcasted_iota(jnp.int32, (2 * heads, cols), 1) // size,
        1.0, 0.0,
    ).astype(BF16)

    def halves(v):
        return [part.astype(F32) for part in split2(v)]

    turned = jnp.transpose(jnp.concatenate(halves(step[...] * ends) + [cum_rows], axis=0))
    cum = turned[:, 2 * heads :]
    write_scale[...] = dot(turned[:, : 2 * heads].astype(BF16), spread)

    def slab(k):
        return pl.ds(pl.multiple_of(k * LANES, LANES), LANES)

    wide = 2 * LANES

    def main_conv(side):
        for j in range(half // 2):
            part = pl.ds(pl.multiple_of(side * half * LANES + j * wide, wide), wide)
            xc[:, part] = conv(x[:, part], taps_x[:, part], moves, x[:, part])

    def first_conv(side):
        part = pl.ds(pl.multiple_of(side * half * LANES, half * LANES), half * LANES)
        head_x = x[:TAIL, part]
        xc[:TAIL, part] = conv(
            head_x, taps_x[:, part], first_moves, jnp.concatenate([edge_x[:, part], head_x], axis=0)
        )

    loads[0].wait()
    bcc[...] = conv(bc[...], taps_bc[...], moves, bc[...])
    loads[1].wait()
    main_conv(1 - odd)

    @pl.when(me > 0)
    def _():
        for copy in edges:
            copy.wait_recv()

    before = edge_docs[...].astype(F32)
    first = jnp.concatenate([before[:, rows - TAIL :], doc_row[:, :TAIL]], axis=1)
    first_gap = (
        lax.broadcasted_iota(jnp.int32, (TAIL, 2 * TAIL), 0)
        + TAIL
        - lax.broadcasted_iota(jnp.int32, (TAIL, 2 * TAIL), 1)
    )
    first_same = doc_col[:TAIL, : 2 * TAIL] == jnp.broadcast_to(first, (TAIL, 2 * TAIL))
    first_moves = [
        jnp.where(first_same & (first_gap == k), 1.0, 0.0).astype(BF16) for k in range(1, taps)
    ]
    head_bc = bc[:TAIL]
    bcc[:TAIL] = conv(head_bc, taps_bc[...], first_moves, jnp.concatenate([edge_bc[...], head_bc], axis=0))
    first_conv(1 - odd)
    b_turned = jnp.transpose(bcc[:, :states].astype(F32)).astype(BF16)
    c_rows = bcc[:, states:]

    entry_rows = jnp.where(doc_row == before[:, rows - 1 :], jnp.exp(cum_rows), 0.0)
    entry = jnp.transpose(jnp.concatenate(halves(entry_rows), axis=0)).astype(BF16)
    through_row = dot(entry[rows - TAIL :], spread)[TAIL - 1 :]
    low_row = lax.broadcasted_iota(jnp.int32, (TAIL, LANES), 0) >= 8

    def pick(c, side):
        at = [through_row[:, (s * half + c) * LANES : (s * half + c + 1) * LANES] for s in (0, 1)]
        return jnp.where(jnp.full((1, LANES), side, jnp.int32) == 1, at[1], at[0])

    def local_state(k):
        written = (xc[:, slab(k)].astype(F32) * write_scale[:, slab(k)]).astype(BF16)
        return dot(b_turned, written)

    pairs, shares = [], []
    chains = [[] for _ in range(rounds)]
    for c in range(half):
        pair_out[c, :states] = local_state((1 - odd) * half + c).astype(BF16)
        high, low = halves(jnp.broadcast_to(pick(c, 1 - odd), (TAIL, LANES)))
        pair_out[c, states:] = jnp.where(low_row, low, high).astype(BF16)
        pairs.append(remote(pair_out.at[c], pair_in.at[c], pair_send.at[c], pair_recv.at[c], partner, group))
        shares.append(remote(share_out.at[c], share_in.at[c], share_send.at[c], share_recv.at[c], partner, group))
        for r in range(rounds):
            chains[r].append(
                remote(
                    chain_out.at[r, c], chain_in.at[r, c], chain_send.at[r * half + c],
                    chain_recv.at[r * half + c], me + 2, group,
                )
            )
        pairs[c].start()

    @pl.when(me < 2)
    def _():
        chain_in[...] = jnp.zeros_like(chain_in)

    main_conv(odd)
    first_conv(odd)
    for c in range(half):
        local[c] = local_state(odd * half + c)

    enter_scale[...] = dot(entry, spread)
    skip_row = dot(
        jnp.concatenate(split2(jnp.broadcast_to(skip[...], (TAIL, heads))), axis=1), spread
    )[0:1]
    gram = jnp.where(same & (gap >= 0), dot(c_rows, b_turned), 0.0)
    mid = rows // 2
    lane = lax.broadcasted_iota(jnp.int32, (rows, LANES), 1)
    per_slab = LANES // size
    loads[2].wait()

    def inner_slab(j):
        part = pl.ds(j * LANES, LANES)
        values = xc[:, part]
        inner = None
        for i in range(per_slab):
            h = j * per_slab + i
            at = cum[:, h : h + 1]
            minus_row = minus[h : h + 1]
            top = gram[:mid, :mid] * jnp.exp(jnp.minimum(at[:mid] - minus_row[:, :mid], 0.0))
            left = gram[mid:, :mid] * jnp.exp(at[mid:] - minus_row[:, :mid])
            right = gram[mid:, mid:] * jnp.exp(jnp.minimum(at[mid:] - minus_row[:, mid:], 0.0))
            below = jnp.concatenate([left.astype(BF16), right.astype(BF16)], axis=1)
            term = jnp.concatenate([dot(top.astype(BF16), values[:mid]), dot(below, values)], axis=0)
            inner = term if inner is None else jnp.where(lane < i * size, inner, term)
        gate = silu(z[:, part].astype(F32))
        base[:, part] = (inner + skip_row[:, j * LANES : (j + 1) * LANES] * values.astype(F32)) * gate
        enter_scale[:, part] = enter_scale[:, part] * gate

    waiting = list(range(slabs))

    def some_inner(count):
        for _ in range(min(count, len(waiting))):
            inner_slab(waiting.pop(0))

    is_odd = jnp.full((states, LANES), odd, jnp.int32) == 1
    some_inner(slabs // 4)
    through = []
    for c in range(half):
        pairs[c].wait_recv()
        mine = local[c]
        theirs = pair_in[c, :states].astype(F32)
        extra = pair_in[c, states:].astype(F32)
        row_odd = is_odd[:1]
        their_through, my_through = extra[0:1] + extra[8:9], pick(c, odd)
        even_through = jnp.where(row_odd, their_through, my_through)
        odd_through = jnp.where(row_odd, my_through, their_through)
        even_local = jnp.where(is_odd, theirs, mine)
        both = jnp.where(is_odd, mine, theirs) + odd_through * even_local
        chain_out[0, c] = both.astype(BF16)

        @pl.when(me < length - 2)
        def _(c=c):
            chains[0][c].start()

        local[c] = even_local
        pair_local[c] = both
        through.append((even_through, even_through * odd_through))
        some_inner(1)

    for r in range(1, rounds):
        for c in range(half):
            @pl.when(me > 1)
            def _(r=r, c=c):
                chains[r - 1][c].wait_recv()

            chain_out[r, c] = (pair_local[c] + through[c][1] * chain_in[r - 1, c].astype(F32)).astype(BF16)

            @pl.when(me < length - 2)
            def _(r=r, c=c):
                chains[r][c].start()

            if c % 2 == 1:
                some_inner(1)
    some_inner(slabs)

    total = jnp.zeros((rows, LANES), F32)

    def finish(k, entered, total):
        gated = base[:, slab(k)] + dot(c_rows, entered) * enter_scale[:, slab(k)]
        base[:, slab(k)] = gated
        return total + gated * gated

    for c in range(half):
        @pl.when(me > 1)
        def _(c=c):
            chains[rounds - 1][c].wait_recv()

        incoming = chain_in[rounds - 1, c].astype(F32)
        between = local[c] + through[c][0] * incoming
        share_out[c] = jnp.where(is_odd, incoming, between).astype(BF16)
        shares[c].start()
        own_entered[c] = jnp.where(is_odd, between, incoming).astype(BF16)

    for c in range(half):
        total = finish(odd * half + c, own_entered[c], total)
    for c in range(half):
        shares[c].wait_recv()
        total = finish((1 - odd) * half + c, share_in[c], total)

    squares = jnp.sum(jnp.transpose(total), axis=0, keepdims=True)
    squares_out[...] = jnp.broadcast_to(squares, squares_out.shape)
    sums = [
        remote(squares_out, squares_in.at[d], squares_send.at[d], squares_recv.at[d], me, peer)
        for d, peer in enumerate(peers)
    ]
    for copy in sums:
        copy.start()
    for d, copy in enumerate(sums):
        copy.wait_recv()
        squares = squares + squares_in[d, 0:1]
    scale = jnp.transpose(jnp.broadcast_to(lax.rsqrt(squares / (cols * groups) + EPS), (LANES, rows)))
    for j in range(slabs):
        part = pl.ds(j * LANES, LANES)
        out[:, part] = (base[:, part] * scale * gain[:, part]).astype(BF16)

    for copy in sums + pairs + shares:
        copy.wait_send()

    @pl.when(me < length - 2)
    def _():
        for copies in chains:
            for copy in copies:
                copy.wait_send()

    @pl.when(me < length - 1)
    def _():
        for copy in edges:
            copy.wait_send()


def body(x_raw, bc_raw, gate_z, step_size, log_decay, doc_ids, conv_x, conv_bc, skip, norm_gain):
    rows, cols = x_raw.shape
    states = bc_raw.shape[1] // 2
    length, groups = lax.axis_size("seq"), lax.axis_size("head")
    half = cols // LANES // 2
    reach = min(length - 1, min(16 * rows, rows * length // 2) // rows)
    rounds = (reach + 1) // 2
    dma = pltpu.SemaphoreType.DMA
    block = pltpu.VMEM((half, states, LANES), BF16)
    pair = pltpu.VMEM((half, states + TAIL, LANES), BF16)
    chain = pltpu.VMEM((rounds, half, states, LANES), BF16)
    local = pltpu.VMEM((half, states, LANES), F32)
    wide = pltpu.VMEM((rows, cols), F32)
    far = pl.BlockSpec(memory_space=pltpu.HBM)
    return pl.pallas_call(
        functools.partial(kernel, length, groups, rounds),
        out_shape=jax.ShapeDtypeStruct((rows, cols), BF16),
        in_specs=[far] * 3 + [pl.BlockSpec(memory_space=pltpu.VMEM)] * 7,
        out_specs=pl.BlockSpec(memory_space=pltpu.VMEM),
        scratch_shapes=[
            pltpu.VMEM((rows, cols), BF16),
            pltpu.VMEM((rows, 2 * states), BF16),
            pltpu.VMEM((rows, cols), BF16),
            dma((3,)),
            pltpu.VMEM((rows, cols), BF16),
            pltpu.VMEM((rows, 2 * states), BF16),
            wide, wide, wide, local, local,
            pltpu.VMEM((TAIL, cols), BF16),
            pltpu.VMEM((TAIL, 2 * states), BF16),
            pltpu.VMEM((1, rows), jnp.int32),
            pair, pair, chain, chain, block, block, block,
            pltpu.VMEM((8, rows), F32),
            pltpu.VMEM((groups - 1, 8, rows), F32),
            dma((3,)), dma((3,)),
            dma((half,)), dma((half,)), dma((rounds * half,)), dma((rounds * half,)), dma((half,)), dma((half,)),
            dma((groups - 1,)), dma((groups - 1,)),
        ],
        compiler_params=pltpu.CompilerParams(
            collective_id=0, has_side_effects=True, vmem_limit_bytes=40 * 1024 * 1024
        ),
        cost_estimate=pl.CostEstimate(flops=10**9, bytes_accessed=2 * 10**6, transcendentals=10**6),
    )(
        x_raw, bc_raw, gate_z, step_size.T, log_decay.T, doc_ids.reshape(1, rows),
        conv_x, conv_bc, skip.reshape(1, -1), norm_gain.reshape(1, -1),
    )


def solution(mesh):
    return jax.shard_map(
        body,
        mesh=mesh,
        in_specs=(
            P("seq", "head"),
            P("seq", None),
            P("seq", "head"),
            P("seq", "head"),
            P("seq", "head"),
            P("seq"),
            P(None, "head"),
            P(),
            P("head"),
            P("head"),
        ),
        out_specs=P("seq", "head"),
        check_vma=False,
    )
```

time: 29.2 us -> 29.5 us (1.010)
  the two profiles are of different devices: /device:TPU:29 before, /device:TPU:25 now
where the time goes in v2:
time: 29.5 us; the launch traced here: 29.1 us
  Pallas kernels  21.7 us (74%)
  local copies, waits for them, and re-layouts  7.29 us (25%)
    pallas_call x1, Pallas kernels, body(): pl.pallas_call(functools.partial(kernel, length, groups, rounds), out_sha...  21.7 us
    unnamed x21, local copies, waits for them, and re-layouts  7.29 us

profile of v2, /device:TPU:25, one launch (start us, length us, event | category | flops | bytes accessed | tf_op | source)
XLA Modules:
  0.0 29.1 jit_solution(5055866359968262000)
XLA Ops:
  0.0 0.0 copy-start.7
  0.0 0.0 copy-start.6
  0.0 0.0 copy-start.8
  0.0 0.7 %copy-done.7 = f32[1024]{0:T(1024)S(1)} copy-done((f32[1024]{0:T(1024)S(1)}, f32[1024]{0:T(1024)}, u32[]{:S(2)}) %copy-start.7) | copy-done | bytes 4120
  0.7 0.0 copy-done.6
  0.7 0.0 copy-done.8
  0.7 0.0 copy-start
  0.7 1.0 %copy-done = bf16[256,1024]{1,0:T(8,128)(2,1)S(1)} copy-done((bf16[256,1024]{1,0:T(8,128)(2,1)S(1)}, bf16[256,1024]{1,0:T(8,128)(2,1)}, u32[]{:S(2)}) %copy-start) | copy-done | bytes 524312
  1.8 0.0 copy-start.1
  1.8 1.0 %copy-done.1 = bf16[256,1024]{1,0:T(8,128)(2,1)S(1)} copy-done((bf16[256,1024]{1,0:T(8,128)(2,1)S(1)}, bf16[256,1024]{1,0:T(8,128)(2,1)}, u32[]{:S(2)}) %copy-start.1) | copy-done | bytes 524312
  2.8 0.0 copy-start.2
  2.8 0.9 %copy-done.2 = bf16[256,256]{1,0:T(8,128)(2,1)S(1)} copy-done((bf16[256,256]{1,0:T(8,128)(2,1)S(1)}, bf16[256,256]{1,0:T(8,128)(2,1)}, u32[]{:S(2)}) %copy-start.2) | copy-done | bytes 131096
  3.7 0.0 copy-start.3
  3.7 0.7 %copy-done.3 = f32[256,16]{0,1:T(8,128)S(1)} copy-done((f32[256,16]{0,1:T(8,128)S(1)}, f32[256,16]{0,1:T(8,128)}, u32[]{:S(2)}) %copy-start.3) | copy-done | bytes 16408
  4.4 0.0 copy-start.4
  4.4 0.7 %copy-done.4 = f32[256,16]{0,1:T(8,128)S(1)} copy-done((f32[256,16]{0,1:T(8,128)S(1)}, f32[256,16]{0,1:T(8,128)}, u32[]{:S(2)}) %copy-start.4) | copy-done | bytes 16408
  5.1 0.0 copy-start.5
  5.1 0.7 %copy-done.5 = f32[4,1024]{1,0:T(4,128)S(1)} copy-done((f32[4,1024]{1,0:T(4,128)S(1)}, f32[4,1024]{1,0:T(4,128)}, u32[]{:S(2)}) %copy-start.5) | copy-done | bytes 16408
  5.9 0.0 copy-start.9
  5.9 0.7 %copy-done.9 = f32[16]{0:T(128)S(1)} copy-done((f32[16]{0:T(128)S(1)}, f32[16]{0:T(128)}, u32[]{:S(2)}) %copy-start.9) | copy-done | bytes 88
  6.5 21.7 %shard_map.100 = bf16[256,1024]{1,0:T(8,128)(2,1)S(1)} custom-call(bf16[256,1024]{1,0:T(8,128)(2,1)S(1)} %copy-done, bf16[256,256]{1,0:T(8,128)(2,1)S(1)} %copy-done.2, bf16[256,1024]{1,0:T(8,128)(2,1)S(1)} %copy-done.1, f32[16,256]{1,0:T(8,128)S(1)} %bitcast.5, f32[16,256]{1,0:T(8,128)S(1)} %bitcast.6, s32[1,256]{1,0:T(1,128)S(1)} %bitcast.8, ...), custom_call_target="tpu_custom_call" | custom-call | flops 1000000000 | bytes 2000000 | tf_op jit(solution)/shard_map/pallas_call | solution.py:368
  28.3 0.8 %copy.12 = bf16[256,1024]{1,0:T(8,128)(2,1)} copy(bf16[256,1024]{1,0:T(8,128)(2,1)S(1)} %shard_map.100) | data formatting | bytes 1048576
Async XLA Ops:
  0.0 0.7 %copy-start.7 = (f32[1024]{0:T(1024)S(1)}, f32[1024]{0:T(1024)}, u32[]{:S(2)}) copy-start(f32[1024]{0:T(1024)} %param.19) | copy-start | bytes 12292
  0.0 0.7 %copy-start.6 = (f32[4,256]{1,0:T(4,128)S(1)}, f32[4,256]{1,0:T(4,128)}, u32[]{:S(2)}) copy-start(f32[4,256]{1,0:T(4,128)} %taps_bc.1) | copy-start | bytes 12292
  0.0 0.7 %copy-start.8 = (s32[256]{0:T(256)S(1)}, s32[256]{0:T(256)}, u32[]{:S(2)}) copy-start(s32[256]{0:T(256)} %param.15) | copy-start | bytes 3076
  0.7 1.0 %copy-start = (bf16[256,1024]{1,0:T(8,128)(2,1)S(1)}, bf16[256,1024]{1,0:T(8,128)(2,1)}, u32[]{:S(2)}) copy-start(bf16[256,1024]{1,0:T(8,128)(2,1)} %x_far.1) | copy-start | bytes 1572868
  1.8 1.0 %copy-start.1 = (bf16[256,1024]{1,0:T(8,128)(2,1)S(1)}, bf16[256,1024]{1,0:T(8,128)(2,1)}, u32[]{:S(2)}) copy-start(bf16[256,1024]{1,0:T(8,128)(2,1)} %z_far.1) | copy-start | bytes 1572868
  2.8 0.9 %copy-start.2 = (bf16[256,256]{1,0:T(8,128)(2,1)S(1)}, bf16[256,256]{1,0:T(8,128)(2,1)}, u32[]{:S(2)}) copy-start(bf16[256,256]{1,0:T(8,128)(2,1)} %bc_far.1) | copy-start | bytes 393220
  3.7 0.7 %copy-start.3 = (f32[256,16]{0,1:T(8,128)S(1)}, f32[256,16]{0,1:T(8,128)}, u32[]{:S(2)}) copy-start(f32[256,16]{0,1:T(8,128)} %param.13) | copy-start | bytes 49156
  4.4 0.7 %copy-start.4 = (f32[256,16]{0,1:T(8,128)S(1)}, f32[256,16]{0,1:T(8,128)}, u32[]{:S(2)}) copy-start(f32[256,16]{0,1:T(8,128)} %param.14) | copy-start | bytes 49156
  5.1 0.7 %copy-start.5 = (f32[4,1024]{1,0:T(4,128)S(1)}, f32[4,1024]{1,0:T(4,128)}, u32[]{:S(2)}) copy-start(f32[4,1024]{1,0:T(4,128)} %taps_x.1) | copy-start | bytes 49156
  5.9 0.7 %copy-start.9 = (f32[16]{0:T(128)S(1)}, f32[16]{0:T(128)}, u32[]{:S(2)}) copy-start(f32[16]{0:T(128)} %param.18) | copy-start | bytes 196

commit v3 on v2

--- a/solution.py
+++ b/solution.py
@@ -389,7 +389,7 @@
             dma((groups - 1,)), dma((groups - 1,)),
         ],
         compiler_params=pltpu.CompilerParams(
-            collective_id=0, has_side_effects=True, vmem_limit_bytes=40 * 1024 * 1024
+            collective_id=0, has_side_effects=True, vmem_limit_bytes=62 * 1024 * 1024
         ),
         cost_estimate=pl.CostEstimate(flops=10**9, bytes_accessed=2 * 10**6, transcendentals=10**6),
     )(

time: 29.5 us -> 25.4 us (0.86)
  local copies, waits for them, and re-layouts: 7.29 us -> 1.87 us
  Pallas kernels: 21.7 us -> 23.3 us
    unnamed x21 -> x1, local copies, waits for them, and re-layouts: 7.29 us -> 1.87 us
    pallas_call x1, Pallas kernels: 21.7 us -> 23.3 us  [body(): pl.pallas_call(functools.partial(kernel, length, groups, rounds), out_sha...]
where the time goes in v3:
time: 25.4 us; the launch traced here: 25.2 us
  Pallas kernels  23.3 us (92%)
  local copies, waits for them, and re-layouts  1.87 us (7%)
    pallas_call x1, Pallas kernels, body(): pl.pallas_call(functools.partial(kernel, length, groups, rounds), out_sha...  23.3 us
    unnamed x1, local copies, waits for them, and re-layouts  1.87 us

profile of v3, /device:TPU:25, one launch (start us, length us, event | category | flops | bytes accessed | tf_op | source)
XLA Modules:
  0.0 25.2 jit_solution(12481238666985693283)
XLA Ops:
  0.0 23.3 %shard_map.100 = bf16[256,1024]{1,0:T(8,128)(2,1)} custom-call(bf16[256,1024]{1,0:T(8,128)(2,1)} %x_far.1, bf16[256,256]{1,0:T(8,128)(2,1)} %bc_far.1, bf16[256,1024]{1,0:T(8,128)(2,1)} %z_far.1, f32[16,256]{1,0:T(8,128)} %bitcast.5, f32[16,256]{1,0:T(8,128)} %bitcast.6, s32[1,256]{1,0:T(1,128)} %bitcast.8, f32[4,1024]{1,0:T(4,128)} %taps_x.1, ...), custom_call_target="tpu_custom_call" | custom-call | flops 1000000000 | bytes 2000000 | tf_op jit(solution)/shard_map/pallas_call | solution.py:368
  23.3 1.9 %copy.12 = bf16[256,1024]{1,0:T(8,128)(2,1)} copy(bf16[256,1024]{1,0:T(8,128)(2,1)} %shard_map.100) | data formatting | bytes 1048576

commit v4 on v3

--- a/solution.py
+++ b/solution.py
@@ -36,9 +36,9 @@
 
 def kernel(
     length, groups, rounds,
-    x_far, bc_far, z_far, step, decay, docs, taps_x, taps_bc, skip, gain,
-    out,
-    x, bc, z, load_sem,
+    x_far, bc_far, z_far, step_far, decay_far, docs_far, taps_x_far, taps_bc_far, skip_far, gain_far,
+    out_far,
+    x, bc, z, step, decay, docs, taps_x, taps_bc, skip, gain, out, load_sem, store_sem,
     xc, bcc, base, enter_scale, write_scale, local, pair_local,
     edge_x, edge_bc, edge_docs,
     pair_out, pair_in, chain_out, chain_in, share_out, share_in, own_entered,
@@ -59,13 +59,6 @@
     partner = me + 1 - 2 * odd
     peers = [(group + d) % groups for d in range(1, groups)]
 
-    loads = [
-        pltpu.make_async_copy(far, here, load_sem.at[i])
-        for i, (far, here) in enumerate(((bc_far, bc), (x_far, x), (z_far, z)))
-    ]
-    for copy in loads:
-        copy.start()
-
     barrier = pltpu.get_barrier_semaphore()
     near = (
         (me > 0, me - 1), (me < length - 1, me + 1), (me > 1, me - 2), (me < length - 2, me + 2),
@@ -78,6 +71,16 @@
     for peer in peers:
         pl.semaphore_signal(barrier, inc=1, device_id=(me, peer), device_id_type=MESH)
 
+    order = (
+        (docs_far, docs), (decay_far, decay), (step_far, step), (bc_far, bc), (taps_bc_far, taps_bc),
+        (x_far, x), (taps_x_far, taps_x), (skip_far, skip), (z_far, z), (gain_far, gain),
+    )
+    loads = [
+        pltpu.make_async_copy(far, here, load_sem.at[i]) for i, (far, here) in enumerate(order)
+    ]
+    for copy in loads:
+        copy.start()
+
     def remote(src, dst, send, recv, seq, head):
         return pltpu.make_async_remote_copy(
             src_ref=src, dst_ref=dst, send_sem=send, recv_sem=recv,
@@ -93,7 +96,7 @@
     edges = [
         remote(x_far.at[pl.ds(rows - TAIL, TAIL)], edge_x, edge_send.at[0], edge_recv.at[0], me + 1, group),
         remote(bc_far.at[pl.ds(rows - TAIL, TAIL)], edge_bc, edge_send.at[1], edge_recv.at[1], me + 1, group),
-        remote(docs, edge_docs, edge_send.at[2], edge_recv.at[2], me + 1, group),
+        remote(docs_far, edge_docs, edge_send.at[2], edge_recv.at[2], me + 1, group),
     ]
 
     @pl.when(me < length - 1)
@@ -107,6 +110,8 @@
         edge_bc[...] = jnp.zeros_like(edge_bc)
         edge_docs[...] = jnp.full(edge_docs.shape, -1, jnp.int32)
 
+    for copy in loads[:3]:
+        copy.wait()
     doc_row = docs[...].astype(F32)
     doc_col = jnp.transpose(jnp.broadcast_to(doc_row, (LANES, rows)))
     same = jnp.concatenate([doc_col] * (rows // LANES), axis=1) == jnp.broadcast_to(doc_row, (rows, rows))
@@ -155,9 +160,11 @@
             head_x, taps_x[:, part], first_moves, jnp.concatenate([edge_x[:, part], head_x], axis=0)
         )
 
-    loads[0].wait()
+    for copy in loads[3:5]:
+        copy.wait()
     bcc[...] = conv(bc[...], taps_bc[...], moves, bc[...])
-    loads[1].wait()
+    for copy in loads[5:7]:
+        copy.wait()
     main_conv(1 - odd)
 
     @pl.when(me > 0)
@@ -222,6 +229,7 @@
         local[c] = local_state(odd * half + c)
 
     enter_scale[...] = dot(entry, spread)
+    loads[7].wait()
     skip_row = dot(
         jnp.concatenate(split2(jnp.broadcast_to(skip[...], (TAIL, heads))), axis=1), spread
     )[0:1]
@@ -229,7 +237,8 @@
     mid = rows // 2
     lane = lax.broadcasted_iota(jnp.int32, (rows, LANES), 1)
     per_slab = LANES // size
-    loads[2].wait()
+    for copy in loads[8:]:
+        copy.wait()
 
     def inner_slab(j):
         part = pl.ds(j * LANES, LANES)
@@ -332,10 +341,19 @@
         copy.wait_recv()
         squares = squares + squares_in[d, 0:1]
     scale = jnp.transpose(jnp.broadcast_to(lax.rsqrt(squares / (cols * groups) + EPS), (LANES, rows)))
+    stores = []
     for j in range(slabs):
         part = pl.ds(j * LANES, LANES)
         out[:, part] = (base[:, part] * scale * gain[:, part]).astype(BF16)
-
+        if j % 2 == 1:
+            done = pl.ds((j - 1) * LANES, 2 * LANES)
+            stores.append(
+                pltpu.make_async_copy(out.at[:, done], out_far.at[:, done], store_sem.at[j // 2])
+            )
+            stores[-1].start()
+
+    for copy in stores:
+        copy.wait()
     for copy in sums + pairs + shares:
         copy.wait_send()
 
@@ -364,17 +382,25 @@
     chain = pltpu.VMEM((rounds, half, states, LANES), BF16)
     local = pltpu.VMEM((half, states, LANES), F32)
     wide = pltpu.VMEM((rows, cols), F32)
+    steps = pltpu.VMEM((step_size.shape[1], rows), F32)
     far = pl.BlockSpec(memory_space=pltpu.HBM)
     return pl.pallas_call(
         functools.partial(kernel, length, groups, rounds),
         out_shape=jax.ShapeDtypeStruct((rows, cols), BF16),
-        in_specs=[far] * 3 + [pl.BlockSpec(memory_space=pltpu.VMEM)] * 7,
-        out_specs=pl.BlockSpec(memory_space=pltpu.VMEM),
+        in_specs=[far] * 10,
+        out_specs=far,
         scratch_shapes=[
             pltpu.VMEM((rows, cols), BF16),
             pltpu.VMEM((rows, 2 * states), BF16),
             pltpu.VMEM((rows, cols), BF16),
-            dma((3,)),
+            steps, steps,
+            pltpu.VMEM((1, rows), jnp.int32),
+            pltpu.VMEM(conv_x.shape, F32),
+            pltpu.VMEM(conv_bc.shape, F32),
+            pltpu.VMEM((1, step_size.shape[1]), F32),
+            pltpu.VMEM((1, cols), F32),
+            pltpu.VMEM((rows, cols), BF16),
+            dma((10,)), dma((half,)),
             pltpu.VMEM((rows, cols), BF16),
             pltpu.VMEM((rows, 2 * states), BF16),
             wide, wide, wide, local, local,

time: 25.4 us -> 24.7 us (0.972)
  Pallas kernels: 23.3 us -> 22.6 us
    pallas_call x1, Pallas kernels: 23.3 us -> 22.6 us  [body(): pl.pallas_call(functools.partial(kernel, length, groups, rounds), out_sha...]
where the time goes in v4:
time: 24.7 us; the launch traced here: 24.5 us
  Pallas kernels  22.6 us (91%)
  local copies, waits for them, and re-layouts  1.87 us (8%)
    pallas_call x1, Pallas kernels, body(): pl.pallas_call(functools.partial(kernel, length, groups, rounds), out_sha...  22.6 us
    unnamed x1, local copies, waits for them, and re-layouts  1.87 us

profile of v4, /device:TPU:25, one launch (start us, length us, event | category | flops | bytes accessed | tf_op | source)
XLA Modules:
  0.0 24.5 jit_solution(14693893610534519408)
XLA Ops:
  0.0 22.6 %shard_map.100 = bf16[256,1024]{1,0:T(8,128)(2,1)} custom-call(bf16[256,1024]{1,0:T(8,128)(2,1)} %x_far.1, bf16[256,256]{1,0:T(8,128)(2,1)} %bc_far.1, bf16[256,1024]{1,0:T(8,128)(2,1)} %z_far.1, f32[16,256]{1,0:T(8,128)} %bitcast.5, f32[16,256]{1,0:T(8,128)} %bitcast.6, s32[1,256]{1,0:T(1,128)} %bitcast.8, f32[4,1024]{1,0:T(4,128)} %taps_x_far.1, ...), custom_call_target="tpu_custom_call" | custom-call | flops 1000000000 | bytes 2000000 | tf_op jit(solution)/shard_map/pallas_call | solution.py:387
  22.6 1.9 %copy.12 = bf16[256,1024]{1,0:T(8,128)(2,1)} copy(bf16[256,1024]{1,0:T(8,128)(2,1)} %shard_map.100) | data formatting | bytes 1048576
